TPU v7x, 32 devices: a whole 2x2x4 slice. The times are simulated.
32 devices in a mesh: group: 2 (over x), dp: 16 (over z, y, core).
Axes of the slice: x: 2, y: 2, z: 4, core: 2. Of those that a mesh axis runs over, the one named last changes fastest.
Arguments:
- tokens: bfloat16 [4096, 8192], P(('group', 'dp')), parts along dimension 0, may hold values from -6 to 6
- frozen_projection_weight: bfloat16 [8192, 1024], replicated, may hold values from -0.0625 to 0.0625
- adapter_down: bfloat16 [256, 8192, 128], P('group', 'dp'), parts along dimension 0, may hold values from -0.0625 to 0.0625
- adapter_up: bfloat16 [256, 128, 1024], P('group', 'dp'), parts along dimension 0, may hold values from -0.5 to 0.5
- adapter_rank: int32 [256], P('group'), parts along dimension 0, may hold values from 8 to 128, as said below
- request_adapter: int32 [32, 3], P('group'), parts along dimension 0, may hold values from 0 to 127
- request_length: int32 [32, 3], P('group'), parts along dimension 0, may hold values from 1 to 64, 128 in all within a row
Outputs:
- projected: bfloat16 [4096, 1024], P(('group', 'dp')), parts along dimension 0
There are 2 independent parts, one for each index of `group`. A program takes and returns all parts, laid end to end along the dimension named above; an argument that names none is the same for every part. Nothing has to cross between parts.
Inputs may be any that keep to these rules, and one draw needn't show every extreme that they name: `adapter_rank`: ranks are multiples of 8; both 8 and 128 occur in every pool. `request_length`: each row sums to 128.
All inputs are finite; a program needn't handle non-finite values.
Results may differ from a plain program's by a relative error of at most 0.0029.
Values may be sent and summed in bfloat16 or wider, within the bound.
A program may use at most 128 MiB of HBM per device.

v0:
```python
import jax
import jax.numpy as jnp
from jax import lax
from jax.sharding import PartitionSpec as P

RMAX = 128
TOK_DEV = 128
REQ_DEV = 3


adapter_alpha_scale = 32.0


def row_requests(request_length):
    request_ends = jnp.cumsum(request_length, axis=1)
    block_rows = jnp.arange(TOK_DEV, dtype=jnp.int32)
    return jnp.sum(
        (block_rows[None, :, None] >= request_ends[:, None, :]).astype(jnp.int32), axis=2
    )


def finish_rows(base_rows, shrunk, onehot, adapter_ranks, up_panels):
    rank_of_row = jnp.sum(jnp.where(onehot, adapter_ranks[None, :], 0), axis=1)
    within = jnp.arange(RMAX, dtype=jnp.int32)[None, :] < rank_of_row[:, None]
    scaling_factor = adapter_alpha_scale / rank_of_row.astype(jnp.float32)
    scaled = jnp.where(within, shrunk * scaling_factor[:, None], jnp.float32(0.0)).astype(
        jnp.bfloat16
    )
    placed = jnp.where(onehot[:, :, None], scaled[:, None, :], jnp.zeros((), jnp.bfloat16))
    placed = placed.reshape(TOK_DEV, REQ_DEV * RMAX)
    adapter_term = jnp.dot(
        placed, up_panels.reshape(REQ_DEV * RMAX, -1), preferred_element_type=jnp.float32
    )
    return (base_rows + adapter_term).astype(jnp.bfloat16)


def local(
    tokens,
    frozen_projection_weight,
    adapter_down,
    adapter_up,
    adapter_rank,
    request_adapter,
    request_length,
):
    position = lax.axis_index("dp")
    adapter_ids = lax.dynamic_index_in_dim(request_adapter, position, 0, keepdims=False)
    own_lengths = lax.dynamic_index_in_dim(request_length, position, 0, keepdims=False)
    own_ends = jnp.cumsum(own_lengths)
    row_request = jnp.sum(
        (jnp.arange(TOK_DEV, dtype=jnp.int32)[:, None] >= own_ends[None, :]).astype(jnp.int32),
        axis=1,
    )
    onehot = row_request[:, None] == jnp.arange(REQ_DEV, dtype=jnp.int32)[None, :]
    adapter_ranks = jnp.take(adapter_rank, adapter_ids)
    expected_output = request_adapter.T
    columns = lax.all_to_all(tokens, "dp", split_axis=1, concat_axis=0, tiled=True)
    all_requests = row_requests(request_length)
    base_rows = jnp.dot(tokens, frozen_projection_weight, preferred_element_type=jnp.float32)
    block_count = lax.axis_size("dp") * TOK_DEV // TOK_DEV
    row_block = columns
    row_block = row_block.reshape(block_count, TOK_DEV, row_block.shape[1])

    def add_request(request, running):
        panel_rows = jnp.take(adapter_down, jnp.take(request_adapter, request, axis=1), axis=0)
        product = jnp.einsum(
            "ntc,ncr->ntr", row_block, panel_rows, preferred_element_type=jnp.float32
        )
        return running + jnp.where((all_requests == request)[:, :, None], product, jnp.float32(0.0))

    running = lax.fori_loop(
        0, REQ_DEV, add_request, jnp.zeros((block_count, TOK_DEV, RMAX), jnp.float32)
    )
    shrunk = lax.psum_scatter(
        running.reshape(lax.axis_size("dp") * TOK_DEV, RMAX), "dp", scatter_dimension=0, tiled=True
    )
    up_out = jnp.take(adapter_up, expected_output, axis=0)
    up_panels = lax.all_to_all(up_out, "dp", split_axis=1, concat_axis=1, tiled=True)
    up_panels = up_panels.reshape(REQ_DEV, RMAX, -1)
    return finish_rows(base_rows, shrunk, onehot, adapter_ranks, up_panels)


def solution(mesh):
    in_specs = (
        P(("group", "dp"), None),
        P(),
        P("group", "dp", None),
        P("group", "dp", None),
        P("group"),
        P("group", None),
        P("group", None),
    )
    out_specs = P(("group", "dp"), None)
    return jax.shard_map(local, mesh=mesh, in_specs=in_specs, out_specs=out_specs, check_vma=False)
```

profile of v0, /device:TPU:0, one launch (start us, length us, event | category | flops | bytes accessed | tf_op | source)
XLA Modules:
  0.0 182.7 jit_solution(1769530127530724586)
XLA Ops:
  6.5 0.0 copy-start
  6.5 4.2 %copy.37 = bf16[128,8192]{0,1:T(8,128)(2,1)} copy(bf16[128,8192]{1,0:T(8,128)(2,1)} %param.9) | data formatting | bytes 4194304 | tf_op args[0]
  10.8 0.0 copy-start.3
  10.8 0.0 copy-start.2
  10.8 7.6 %all-to-all-start = ((bf16[128,16,512]{0,2,1:T(8,128)(2,1)}), bf16[128,16,512]{0,2,1:T(8,128)(2,1)}, u32[]{:S(2)}, u32[]{:S(2)}) async-start(bf16[128,16,512]{0,2,1:T(8,128)(2,1)} %bitcast.43), calls=%async_computation | async-start | bytes 4194304 | tf_op jit(solution)/shard_map/all_to_all | solution.py:57
  18.4 0.0 copy-done.3
  18.4 0.2 dynamic-slice_reduce_fusion
  18.6 0.0 copy-done.2
  18.6 0.1 constant_dynamic-slice_fusion
  18.7 0.1 copy.44
  18.8 0.2 reduce-window.8
  19.0 0.1 reshape.207
  19.1 0.0 copy-done
  19.1 0.0 copy-start.1
  19.1 0.6 gather_fusion.2
  19.7 0.1 broadcast_select_fusion.1
  19.9 1.0 copy.41
  20.8 0.0 copy-done.1
  20.8 0.6 gather_fusion.1
  21.5 0.1 convert_reduce_fusion.1
  21.6 0.1 convert_reduce_fusion
  21.7 37.9 %all-to-all-done = bf16[128,16,512]{0,2,1:T(8,128)(2,1)} async-done(((bf16[128,16,512]{0,2,1:T(8,128)(2,1)}), bf16[128,16,512]{0,2,1:T(8,128)(2,1)}, u32[]{:S(2)}, u32[]{:S(2)}) %all-to-all-start) | async-done | bytes 2097184 | tf_op jit(solution)/shard_map/all_to_all | solution.py:57
  59.5 11.2 %all-to-all-start.1 = ((bf16[3,16,8,1024]{3,2,0,1:T(8,128)(2,1)}), bf16[3,16,8,1024]{3,2,0,1:T(8,128)(2,1)S(1)}, u32[]{:S(2)}, u32[]{:S(2)}) async-start(bf16[3,16,8,1024]{3,2,0,1:T(8,128)(2,1)} %copy.41), calls=%async_computation.2 | async-start | bytes 1572864 | tf_op jit(solution)/shard_map/all_to_all | solution.py:78
  70.7 0.0 reduce-scatter.2.cloned.1.call-start
  70.8 3.9 %copy.38 = bf16[16,128,512]{2,1,0:T(8,128)(2,1)} copy(bf16[16,128,512]{1,2,0:T(8,128)(2,1)} %bitcast.6) | data formatting | bytes 4194304
  74.7 36.5 %while.15 = (s32[]{:T(128)}, f32[16,128,128]{1,2,0:T(8,128)}, s32[16,128]{1,0:T(8,128)S(1)}, s32[16,3]{0,1:T(4,128)S(1)}, bf16[128,512,128]{2,1,0:T(8,128)(2,1)}...) while((s32[]{:T(128)}, f32[16,128,128]{1,2,0:T(8,128)}, ...), condition=%wide.region_6.7_spmd.clone, body=%wide.region_5.6_spmd.clone.sunk | while | flops 270273728 | bytes 10502634 | solution.py:71
  74.8 7.9 %gather_fusion = bf16[16,512,128]{2,1,0:T(8,128)(2,1)} fusion(bf16[128,512,128]{2,1,0:T(8,128)(2,1)} %get-tuple-element.242, s32[1024]{0:T(1024)S(1)} %pad_clamp_fusion.4), kind=kCustom, calls=%fused_computation.clone.clone.1 | custom fusion | bytes 4194368 | tf_op jit(solution)/shard_map/while/body/eval_jaxpr/jit(_take)/gather | solution.py:65
  82.7 4.1 %fusion.31 = f32[16,128,128]{1,2,0:T(8,128)} fusion(bf16[16,128,512]{2,1,0:T(8,128)(2,1)} %get-tuple-element.243, bf16[16,512,128]{2,1,0:T(8,128)(2,1)} %gather_fusion, pred[16]{0:T(512)(128)(4,1)S(1)} %compare_and_fusion.3, f32[16,128,128]{1,2,0:T(8,128)} %get-tuple-element.230, pred[]{:T(512)S(6)} %compare.4, ...), kind=kOutput, calls=%fused_computation.8.clone.1 | convolution fusion | flops 270270464 | bytes 6293521 | tf_op jit(solution)/shard_map/while/body/eval_jaxpr/ntc,ncr->ntr/dot_general | solution.py:66
  86.8 7.9 %gather_fusion = bf16[16,512,128]{2,1,0:T(8,128)(2,1)} fusion(bf16[128,512,128]{2,1,0:T(8,128)(2,1)} %get-tuple-element.242, s32[1024]{0:T(1024)S(1)} %pad_clamp_fusion.4), kind=kCustom, calls=%fused_computation.clone.clone.1 | custom fusion | bytes 4194368 | tf_op jit(solution)/shard_map/while/body/eval_jaxpr/jit(_take)/gather | solution.py:65
  94.7 4.3 %fusion.31 = f32[16,128,128]{1,2,0:T(8,128)} fusion(bf16[16,128,512]{2,1,0:T(8,128)(2,1)} %get-tuple-element.243, bf16[16,512,128]{2,1,0:T(8,128)(2,1)} %gather_fusion, pred[16]{0:T(512)(128)(4,1)S(1)} %compare_and_fusion.3, f32[16,128,128]{1,2,0:T(8,128)} %get-tuple-element.230, pred[]{:T(512)S(6)} %compare.4, ...), kind=kOutput, calls=%fused_computation.8.clone.1 | convolution fusion | flops 270270464 | bytes 6293521 | tf_op jit(solution)/shard_map/while/body/eval_jaxpr/ntc,ncr->ntr/dot_general | solution.py:66
  99.0 7.9 %gather_fusion = bf16[16,512,128]{2,1,0:T(8,128)(2,1)} fusion(bf16[128,512,128]{2,1,0:T(8,128)(2,1)} %get-tuple-element.242, s32[1024]{0:T(1024)S(1)} %pad_clamp_fusion.4), kind=kCustom, calls=%fused_computation.clone.clone.1 | custom fusion | bytes 4194368 | tf_op jit(solution)/shard_map/while/body/eval_jaxpr/jit(_take)/gather | solution.py:65
  106.9 4.3 %fusion.31 = f32[16,128,128]{1,2,0:T(8,128)} fusion(bf16[16,128,512]{2,1,0:T(8,128)(2,1)} %get-tuple-element.243, bf16[16,512,128]{2,1,0:T(8,128)(2,1)} %gather_fusion, pred[16]{0:T(512)(128)(4,1)S(1)} %compare_and_fusion.3, f32[16,128,128]{1,2,0:T(8,128)} %get-tuple-element.230, pred[]{:T(512)S(6)} %compare.4, ...), kind=kOutput, calls=%fused_computation.8.clone.1 | convolution fusion | flops 270270464 | bytes 6293521 | tf_op jit(solution)/shard_map/while/body/eval_jaxpr/ntc,ncr->ntr/dot_general | solution.py:66
  111.3 2.5 %copy.39 = f32[16,128,128]{2,1,0:T(8,128)} copy(f32[16,128,128]{1,2,0:T(8,128)} %get-tuple-element.114) | data formatting | bytes 2097152 | tf_op jit(solution)/shard_map/while | solution.py:71
  113.8 0.0 reduce-scatter.2.cloned.1.call-update
  113.9 0.1 select_reduce_fusion
  113.9 8.7 %fusion.18 = f32[128,1024]{1,0:T(8,128)S(1)} fusion(bf16[128,8192]{1,0:T(8,128)(2,1)} %param.9, bf16[8192,1024]{1,0:T(8,128)(2,1)} %param.10), kind=kOutput, calls=%fused_computation.42 | convolution fusion | flops 2147483648 | bytes 19398656 | tf_op jit(solution)/shard_map/dot_general | solution.py:59
  122.7 0.0 all-to-all-done.1
  122.7 1.0 copy.42
  123.7 49.0 %reduce-scatter.2.cloned.1.call-done = f32[128,128]{1,0:T(8,128)} async-done(((f32[2048,128]{1,0:T(8,128)}), f32[128,128]{1,0:T(8,128)}) %reduce-scatter.2.cloned.1.call-update) | async-done | bytes 65552 | tf_op jit(solution)/shard_map/reduce_scatter | solution.py:74
  172.6 0.9 select_convert_fusion
  173.6 0.1 copy.40
  173.7 2.2 %fusion.15 = bf16[128,1024]{1,0:T(8,128)(2,1)} fusion(f32[128,1024]{1,0:T(8,128)S(1)} %fusion.18, bf16[128,384]{0,1:T(8,128)(2,1)S(1)} %bitcast.47, bf16[384,1024]{1,0:T(8,128)(2,1)} %bitcast.45), kind=kOutput, calls=%fused_computation.19 | convolution fusion | flops 100925440 | bytes 1671168 | tf_op jit(solution)/shard_map/dot_general | solution.py:31
  (23 shorter events, 0.2 us)
Async XLA Ops:
  6.5 12.5 %copy-start = (bf16[128,8,1024]{2,1,0:T(8,128)(2,1)S(1)}, bf16[128,8,1024]{2,1,0:T(8,128)(2,1)}, u32[]{:S(2)}) copy-start(bf16[128,8,1024]{2,1,0:T(8,128)(2,1)} %param.12) | copy-start | bytes 6291460
  10.8 7.6 %copy-start.3 = (s32[16,3]{0,1:T(4,128)S(1)}, s32[16,3]{0,1:T(4,128)}, u32[]{:S(2)}) copy-start(s32[16,3]{0,1:T(4,128)} %param.15) | copy-start | bytes 580
  10.8 7.8 %copy-start.2 = (s32[16,3]{0,1:T(4,128)S(1)}, s32[16,3]{0,1:T(4,128)}, u32[]{:S(2)}) copy-start(s32[16,3]{0,1:T(4,128)} %param.14) | copy-start | bytes 580
  10.8 48.7 %all-to-all-start = ((bf16[128,16,512]{0,2,1:T(8,128)(2,1)}), bf16[128,16,512]{0,2,1:T(8,128)(2,1)}, u32[]{:S(2)}, u32[]{:S(2)}) async-start(bf16[128,16,512]{0,2,1:T(8,128)(2,1)} %bitcast.43), calls=%async_computation | async-start | bytes 4194304 | tf_op jit(solution)/shard_map/all_to_all | solution.py:57
  19.1 1.8 copy-start.1
  59.5 63.2 %all-to-all-start.1 = ((bf16[3,16,8,1024]{3,2,0,1:T(8,128)(2,1)}), bf16[3,16,8,1024]{3,2,0,1:T(8,128)(2,1)S(1)}, u32[]{:S(2)}, u32[]{:S(2)}) async-start(bf16[3,16,8,1024]{3,2,0,1:T(8,128)(2,1)} %copy.41), calls=%async_computation.2 | async-start | bytes 1572864 | tf_op jit(solution)/shard_map/all_to_all | solution.py:78
  70.7 101.9 %reduce-scatter.2.cloned.1.call-start = ((), (), s32[]{:S(2)}) async-start(), calls=%async_computation.3 | async-start | bytes 1114112 | tf_op jit(solution)/shard_map/reduce_scatter | solution.py:74
Sparse Core Ops, SparseCore 0:
  114.0 58.6 reduce-scatter.1
where the time goes:
time: 183 us
  waiting for transfers between devices  86.8 us (47%)
  local copies, waits for them, and re-layouts  38.2 us (21%)
  matrix products  23.6 us (13%)
  starting transfers between devices  18.8 us (10%)
  between operations  13.5 us (7%)
    reduce_scatter x1, waiting for transfers between devices, local(): lax.psum_scatter(running.reshape(lax.axis_size('dp') * TOK_DEV, RMAX), 'd...  49 us
    all_to_all x1, waiting for transfers between devices, local(): lax.all_to_all(tokens, 'dp', split_axis=1, concat_axis=0, tiled=True)  37.9 us
    gather x3, local copies, waits for them, and re-layouts, add_request(): jnp.take(adapter_down, jnp.take(request_adapter, request, axis=1), axis=0)  23.6 us
    dot_general x3, matrix products, add_request(): jnp.einsum('ntc,ncr->ntr', row_block, panel_rows, preferred_element_type=...  12.7 us
    all_to_all x1, starting transfers between devices, local(): lax.all_to_all(up_out, 'dp', split_axis=1, concat_axis=1, tiled=True)  11.2 us
    dot_general x1, matrix products, local(): jnp.dot(tokens, frozen_projection_weight, preferred_element_type=jnp.floa...  8.74 us
    unnamed x11, local copies, waits for them, and re-layouts  8.3 us
    all_to_all x1, starting transfers between devices, local(): lax.all_to_all(tokens, 'dp', split_axis=1, concat_axis=0, tiled=True)  7.57 us
  transfers between devices with their start and end apart: 3, of which 2 were waited for; matrix products, arithmetic and copies ran while one was open for 31% of the time, Pallas kernels for 0%

commit v1 on v0

--- a/solution.py
+++ b/solution.py
@@ -1,7 +1,15 @@
+import functools
+
 import jax
 import jax.numpy as jnp
+import numpy as np
 from jax import lax
+from jax.experimental import pallas as pl
+from jax.experimental.pallas import tpu as pltpu
 from jax.sharding import PartitionSpec as P
+
+MESH = pl.DeviceIdType.MESH
+
 
 RMAX = 128
 TOK_DEV = 128
@@ -80,6 +88,264 @@
     return finish_rows(base_rows, shrunk, onehot, adapter_ranks, up_panels)
 
 
+def flip(me, step, n):
+    total, weight = 0, 1
+    while weight < n:
+        total = total + weight * ((me // weight + step // weight) % 2)
+        weight *= 2
+    return total
+
+
+def fused(
+    n, req, spread,
+    adapters, lengths, ranks, tokens, weight, down, up, place, code,
+    out,
+    tok, wgt, dwn, upv, placev, codev, base, tok_in, up_out, up_in, part, got1, got2, got3,
+    load_sem, wgt_sem, tok_send, tok_recv, up_send, up_recv,
+    s1_send, s1_recv, s2_send, s2_recv, s3_send, s3_recv,
+):
+    me = lax.axis_index("dp")
+    rows, width = tokens.shape
+    chunk = width // n
+    rank_rows = up.shape[1]
+    half = up.shape[2] // 2
+
+    loads = [
+        pltpu.make_async_copy(up, upv, load_sem.at[0]),
+        pltpu.make_async_copy(tokens, tok, load_sem.at[1]),
+        pltpu.make_async_copy(down, dwn, load_sem.at[2]),
+        pltpu.make_async_copy(place, placev, load_sem.at[3]),
+        pltpu.make_async_copy(code, codev, load_sem.at[4]),
+    ]
+
+    def weight_copy(c):
+        piece = pl.ds(pl.multiple_of(c * chunk, chunk), chunk)
+        return pltpu.make_async_copy(weight.at[piece], wgt.at[piece], wgt_sem.at[c])
+
+    def token_copy(step):
+        peer = flip(me, step, n)
+        return pltpu.make_async_remote_copy(
+            src_ref=tokens.at[:, pl.ds(pl.multiple_of(peer * chunk, chunk), chunk)],
+            dst_ref=tok_in.at[step],
+            send_sem=tok_send.at[step], recv_sem=tok_recv.at[step],
+            device_id={"dp": peer}, device_id_type=MESH,
+        )
+
+    def up_copy(step):
+        peer = flip(me, step, n)
+        return pltpu.make_async_remote_copy(
+            src_ref=up_out.at[peer], dst_ref=up_in.at[me],
+            send_sem=up_send.at[step], recv_sem=up_recv.at[step],
+            device_id={"dp": peer}, device_id_type=MESH,
+        )
+
+    def up_arrival(step):
+        peer = flip(me, step, n)
+        return pltpu.make_async_remote_copy(
+            src_ref=up_out.at[peer], dst_ref=up_in.at[peer],
+            send_sem=up_send.at[step], recv_sem=up_recv.at[step],
+            device_id={"dp": peer}, device_id_type=MESH,
+        )
+
+    barrier = pltpu.get_barrier_semaphore()
+
+    def greet(step, carry):
+        pl.semaphore_signal(barrier, inc=1, device_id={"dp": flip(me, step, n)}, device_id_type=MESH)
+        return carry
+
+    lax.fori_loop(1, n, greet, 0)
+    loads[0].start()
+    loads[1].start()
+
+    def start_weight(c, carry):
+        weight_copy(c).start()
+        return carry
+
+    lax.fori_loop(0, n, start_weight, 0)
+    for load in loads[2:]:
+        load.start()
+    pl.semaphore_wait(barrier, n - 1)
+
+    def send_tokens(i, carry):
+        token_copy(n - 1 - i).start()
+        return carry
+
+    lax.fori_loop(0, n - 1, send_tokens, 0)
+
+    loads[0].wait()
+
+    def pick_up(i, carry):
+        panels = [upv[adapters[i, q]].astype(jnp.float32) for q in range(req)]
+        picked = [p[:, h * half:(h + 1) * half] for h in range(2) for p in panels]
+        up_out[i] = jnp.concatenate(picked, axis=0).astype(jnp.bfloat16)
+        return carry
+
+    lax.fori_loop(0, n, pick_up, 0)
+    up_in[me] = up_out[me]
+
+    def send_up(i, carry):
+        up_copy(n - 1 - i).start()
+        return carry
+
+    lax.fori_loop(0, n - 1, send_up, 0)
+
+    loads[1].wait()
+    base[...] = jnp.zeros_like(base)
+
+    def add_base(c, carry):
+        weight_copy(c).wait()
+        piece = pl.ds(pl.multiple_of(c * chunk, chunk), chunk)
+        base[...] += jnp.dot(tok[:, piece], wgt[piece, :], preferred_element_type=jnp.float32)
+        return carry
+
+    lax.fori_loop(0, n, add_base, 0)
+    for load in loads[2:]:
+        load.wait()
+    tok_in[0] = tok[:, pl.ds(pl.multiple_of(me * chunk, chunk), chunk)]
+
+    row = lax.broadcasted_iota(jnp.int32, (rows, 1), 0)
+
+    def shrink(step):
+        i = flip(me, step, n)
+        block = tok_in[step]
+        total = jnp.dot(block, dwn[adapters[i, 0]], preferred_element_type=jnp.float32)
+        end = jnp.int32(0)
+        for q in range(1, req):
+            end = end + lengths[i, q - 1]
+            product = jnp.dot(block, dwn[adapters[i, q]], preferred_element_type=jnp.float32)
+            total = jnp.where(row >= end, product, total)
+        part[step] = total
+
+    def sum_copy(src, dst, sends, recvs, slot, peer):
+        return pltpu.make_async_remote_copy(
+            src_ref=src, dst_ref=dst, send_sem=sends.at[slot], recv_sem=recvs.at[slot],
+            device_id={"dp": peer}, device_id_type=MESH,
+        )
+
+    waiting = []
+    for m in range(n // 4):
+        def one(step, carry):
+            @pl.when(step > 0)
+            def _():
+                token_copy(step).wait_recv()
+            shrink(step)
+            return carry
+
+        lax.fori_loop(4 * m, 4 * m + 4, one, 0)
+        first = [
+            sum_copy(part.at[2 * k + 1], got1.at[k], s1_send, s1_recv, k, flip(me, 1, n))
+            for k in (2 * m, 2 * m + 1)
+        ]
+        for copy in first:
+            copy.start()
+        for k, copy in zip((2 * m + 1, 2 * m), reversed(first)):
+            copy.wait_recv()
+            part[2 * k] = part[2 * k] + got1[k]
+            if k % 2:
+                second = sum_copy(part.at[2 * k], got2.at[m], s2_send, s2_recv, m, flip(me, 2, n))
+                second.start()
+        second.wait_recv()
+        part[4 * m] = part[4 * m] + got2[m]
+        waiting += first + [second]
+        if m:
+            third = sum_copy(part.at[4 * m], got3.at[m], s3_send, s3_recv, m, flip(me, 4 * m, n))
+            third.start()
+            waiting.append(third)
+
+    shrunk = part[0]
+    for m in range(1, n // 4):
+        sum_copy(part.at[4 * m], got3.at[m], s3_send, s3_recv, m, flip(me, 4 * m, n)).wait_recv()
+        shrunk = shrunk + got3[m]
+
+    request = jnp.zeros((rows, 1), jnp.int32)
+    rank = jnp.zeros((rows, 1), jnp.int32) + ranks[adapters[me, 0]]
+    end = jnp.int32(0)
+    for q in range(1, req):
+        end = end + lengths[me, q - 1]
+        later = row >= end
+        request = jnp.where(later, q, request)
+        rank = jnp.where(later, ranks[adapters[me, q]], rank)
+    within = lax.broadcasted_iota(jnp.int32, shrunk.shape, 1) < rank
+    factor = 32.0 / rank.astype(jnp.float32)
+    scaled = jnp.where(within, shrunk * factor, 0.0).astype(jnp.bfloat16)
+    spread_out = jnp.dot(scaled, placev[...], preferred_element_type=jnp.float32)
+    codes = codev[0:1, :]
+
+    def await_up(step, carry):
+        up_arrival(step).wait_recv()
+        return carry
+
+    lax.fori_loop(1, n, await_up, 0)
+    panels = up_in[...].reshape(spread, half)
+    for h in range(2):
+        placed = jnp.where(codes == request + h * req, spread_out, 0.0).astype(jnp.bfloat16)
+        term = jnp.dot(placed, panels, preferred_element_type=jnp.float32)
+        piece = slice(h * half, (h + 1) * half)
+        out[:, piece] = (base[:, piece] + term).astype(jnp.bfloat16)
+
+    def await_sent(step, carry):
+        token_copy(step).wait_send()
+        up_copy(step).wait_send()
+        return carry
+
+    lax.fori_loop(1, n, await_sent, 0)
+    for copy in waiting:
+        copy.wait_send()
+
+
+def fused_local(tokens, weight, down, up, ranks, adapters, lengths):
+    n = lax.axis_size("dp")
+    rows, width = tokens.shape
+    chunk = width // n
+    columns = weight.shape[1]
+    req = adapters.shape[1]
+    rank_rows, rmax = up.shape[1], down.shape[2]
+    half = columns // 2
+    group = 2 * req * rank_rows
+    spread = n * group
+    slot = np.arange(spread)
+    rank_of = (slot // group) * rank_rows + slot % rank_rows
+    place = jnp.asarray(np.arange(rmax)[:, None] == rank_of[None, :], jnp.bfloat16)
+    code = jnp.asarray(np.tile((slot % group) // rank_rows, (8, 1)), jnp.int32)
+    dma = pltpu.SemaphoreType.DMA
+    smem = pl.BlockSpec(memory_space=pltpu.SMEM)
+    hbm = pl.BlockSpec(memory_space=pl.ANY)
+    return pl.pallas_call(
+        functools.partial(fused, n, req, spread),
+        out_shape=jax.ShapeDtypeStruct((rows, columns), jnp.bfloat16),
+        in_specs=[smem] * 3 + [hbm] * 6,
+        out_specs=pl.BlockSpec(memory_space=pltpu.VMEM),
+        scratch_shapes=[
+            pltpu.VMEM((rows, width), jnp.bfloat16),
+            pltpu.VMEM(weight.shape, jnp.bfloat16),
+            pltpu.VMEM(down.shape, jnp.bfloat16),
+            pltpu.VMEM(up.shape, jnp.bfloat16),
+            pltpu.VMEM(place.shape, jnp.bfloat16),
+            pltpu.VMEM(code.shape, jnp.int32),
+            pltpu.VMEM((rows, columns), jnp.float32),
+            pltpu.VMEM((n, rows, chunk), jnp.bfloat16),
+            pltpu.VMEM((n, group, half), jnp.bfloat16),
+            pltpu.VMEM((n, group, half), jnp.bfloat16),
+            pltpu.VMEM((n, rows, rmax), jnp.float32),
+            pltpu.VMEM((n // 2, rows, rmax), jnp.float32),
+            pltpu.VMEM((n // 4, rows, rmax), jnp.float32),
+            pltpu.VMEM((n // 4, rows, rmax), jnp.float32),
+            dma((5,)), dma((n,)), dma((n,)), dma((n,)), dma((n,)), dma((n,)),
+            dma((n // 2,)), dma((n // 2,)), dma((n // 4,)), dma((n // 4,)), dma((n // 4,)), dma((n // 4,)),
+        ],
+        compiler_params=pltpu.CompilerParams(
+            collective_id=0, has_side_effects=True, vmem_limit_bytes=56 * 1024 * 1024
+        ),
+        cost_estimate=pl.CostEstimate(flops=3 * 10**9, bytes_accessed=4 * 10**7, transcendentals=0),
+    )(adapters, lengths, ranks, tokens, weight, down, up, place, code)
+
+
+def fits(mesh, tokens, up):
+    n = mesh.shape["dp"]
+    chunk, rank_rows = tokens.shape[1] // n, up.shape[1] // n
+    return n >= 8 and n & (n - 1) == 0 and n <= 32 and chunk % 128 == 0 and rank_rows % 8 == 0
+
+
 def solution(mesh):
     in_specs = (
         P(("group", "dp"), None),
@@ -91,4 +357,9 @@
         P("group", None),
     )
     out_specs = P(("group", "dp"), None)
-    return jax.shard_map(local, mesh=mesh, in_specs=in_specs, out_specs=out_specs, check_vma=False)
+
+    def run(*arrays):
+        body = fused_local if fits(mesh, arrays[0], arrays[3]) else local
+        return jax.shard_map(body, mesh=mesh, in_specs=in_specs, out_specs=out_specs, check_vma=False)(*arrays)
+
+    return run

time: 183 us -> 90.4 us (0.49)
  waiting for transfers between devices: 86.8 us -> 0 us
  Pallas kernels: 0 us -> 85.8 us
  local copies, waits for them, and re-layouts: 38.2 us -> 4.37 us
  matrix products: 23.6 us -> 0 us
  starting transfers between devices: 18.8 us -> 0 us
  between operations: 13.5 us -> 0.01 us
    pallas_call x0 -> x1, Pallas kernels: none -> 85.8 us  [fused_local(): pl.pallas_call(functools.partial(fused, n, req, spread), out_shape=jax.Sh...]
    reduce_scatter x1 -> x0, waiting for transfers between devices: 49 us -> none  [local(): lax.psum_scatter(running.reshape(lax.axis_size('dp') * TOK_DEV, RMAX), 'd...]
    all_to_all x2 -> x0, waiting for transfers between devices: 37.9 us -> none  [the longest x1 37.9 us: local(): lax.all_to_all(tokens, 'dp', split_axis=1, concat_axis=0, tiled=True)]
    gather x5 -> x0, local copies, waits for them, and re-layouts: 24.9 us -> none  [the longest x3 23.6 us: add_request(): jnp.take(adapter_down, jnp.take(request_adapter, request, axis=1), axis=0)]
    dot_general x5 -> x0, matrix products: 23.6 us -> none  [the longest x3 12.7 us: add_request(): jnp.einsum('ntc,ncr->ntr', row_block, panel_rows, preferred_element_type=...]
    all_to_all x2 -> x0, starting transfers between devices: 18.8 us -> none  [the longest x1 11.2 us: local(): lax.all_to_all(up_out, 'dp', split_axis=1, concat_axis=1, tiled=True)]
    unnamed x11 -> x3, local copies, waits for them, and re-layouts: 8.3 us -> 4.37 us
    while x1 -> x0, local copies, waits for them, and re-layouts: 2.55 us -> none  [local(): lax.fori_loop(0, REQ_DEV, add_request, jnp.zeros((block_count, TOK_DEV, R...]
  transfers between devices with their start and end apart: 3 -> 0, of which waited for: 2 -> 0; matrix products, arithmetic and copies ran while one was open for 31% -> 0% of each run, Pallas kernels for 0% -> 0%
where the time goes in v1:
time: 90.4 us; the launch traced here: 90.2 us
  Pallas kernels  85.8 us (95%)
  local copies, waits for them, and re-layouts  4.37 us (5%)
    pallas_call x1, Pallas kernels, fused_local(): pl.pallas_call(functools.partial(fused, n, req, spread), out_shape=jax.Sh...  85.8 us
    unnamed x3, local copies, waits for them, and re-layouts  4.37 us

profile of v1, /device:TPU:0, one launch (start us, length us, event | category | flops | bytes accessed | tf_op | source)
XLA Modules:
  0.0 90.2 jit_solution(4330864263656609530)
XLA Ops:
  0.0 1.4 %copy.10.adapters = s32[16,3]{1,0:T(8,128)} copy(s32[16,3]{0,1:T(4,128)} %param.14) | data formatting | bytes 384 | tf_op args[5]
  1.4 1.3 %copy.11.lengths = s32[16,3]{1,0:T(8,128)} copy(s32[16,3]{0,1:T(4,128)} %param.15) | data formatting | bytes 384 | tf_op args[6]
  2.7 85.8 %shard_map.91 = bf16[128,1024]{1,0:T(8,128)(2,1)} custom-call(s32[16,3]{1,0:T(8,128)} %copy.10.adapters, s32[16,3]{1,0:T(8,128)} %copy.11.lengths, s32[128]{0:T(128)} %ranks.1, bf16[128,8192]{1,0:T(8,128)(2,1)} %tokens.1, bf16[8192,1024]{1,0:T(8,128)(2,1)} %weight.1, bf16[128,512,128]{2,1,0:T(8,128)(2,1)} %down.1, bf16[128,8,1024]{2,1,0:T(8,128)(2,1)} %up.1, ...), custom_call_target="tpu_custom_call" | custom-call | flops 3000000000 | bytes 40000000 | tf_op jit(solution)/shard_map/pallas_call | solution.py:313
  88.5 1.7 %copy.13 = bf16[128,1024]{1,0:T(8,128)(2,1)} copy(bf16[128,1024]{1,0:T(8,128)(2,1)} %shard_map.91) | data formatting | bytes 524288

commit v2 on v1

v2 whole, which is shorter than its diff:
```python
import functools

import jax
import jax.numpy as jnp
import numpy as np
from jax import lax
from jax.experimental import pallas as pl
from jax.experimental.pallas import tpu as pltpu
from jax.sharding import PartitionSpec as P

MESH = pl.DeviceIdType.MESH


RMAX = 128
TOK_DEV = 128
REQ_DEV = 3


adapter_alpha_scale = 32.0


def row_requests(request_length):
    request_ends = jnp.cumsum(request_length, axis=1)
    block_rows = jnp.arange(TOK_DEV, dtype=jnp.int32)
    return jnp.sum(
        (block_rows[None, :, None] >= request_ends[:, None, :]).astype(jnp.int32), axis=2
    )


def finish_rows(base_rows, shrunk, onehot, adapter_ranks, up_panels):
    rank_of_row = jnp.sum(jnp.where(onehot, adapter_ranks[None, :], 0), axis=1)
    within = jnp.arange(RMAX, dtype=jnp.int32)[None, :] < rank_of_row[:, None]
    scaling_factor = adapter_alpha_scale / rank_of_row.astype(jnp.float32)
    scaled = jnp.where(within, shrunk * scaling_factor[:, None], jnp.float32(0.0)).astype(
        jnp.bfloat16
    )
    placed = jnp.where(onehot[:, :, None], scaled[:, None, :], jnp.zeros((), jnp.bfloat16))
    placed = placed.reshape(TOK_DEV, REQ_DEV * RMAX)
    adapter_term = jnp.dot(
        placed, up_panels.reshape(REQ_DEV * RMAX, -1), preferred_element_type=jnp.float32
    )
    return (base_rows + adapter_term).astype(jnp.bfloat16)


def local(
    tokens,
    frozen_projection_weight,
    adapter_down,
    adapter_up,
    adapter_rank,
    request_adapter,
    request_length,
):
    position = lax.axis_index("dp")
    adapter_ids = lax.dynamic_index_in_dim(request_adapter, position, 0, keepdims=False)
    own_lengths = lax.dynamic_index_in_dim(request_length, position, 0, keepdims=False)
    own_ends = jnp.cumsum(own_lengths)
    row_request = jnp.sum(
        (jnp.arange(TOK_DEV, dtype=jnp.int32)[:, None] >= own_ends[None, :]).astype(jnp.int32),
        axis=1,
    )
    onehot = row_request[:, None] == jnp.arange(REQ_DEV, dtype=jnp.int32)[None, :]
    adapter_ranks = jnp.take(adapter_rank, adapter_ids)
    expected_output = request_adapter.T
    columns = lax.all_to_all(tokens, "dp", split_axis=1, concat_axis=0, tiled=True)
    all_requests = row_requests(request_length)
    base_rows = jnp.dot(tokens, frozen_projection_weight, preferred_element_type=jnp.float32)
    block_count = lax.axis_size("dp") * TOK_DEV // TOK_DEV
    row_block = columns
    row_block = row_block.reshape(block_count, TOK_DEV, row_block.shape[1])

    def add_request(request, running):
        panel_rows = jnp.take(adapter_down, jnp.take(request_adapter, request, axis=1), axis=0)
        product = jnp.einsum(
            "ntc,ncr->ntr", row_block, panel_rows, preferred_element_type=jnp.float32
        )
        return running + jnp.where((all_requests == request)[:, :, None], product, jnp.float32(0.0))

    running = lax.fori_loop(
        0, REQ_DEV, add_request, jnp.zeros((block_count, TOK_DEV, RMAX), jnp.float32)
    )
    shrunk = lax.psum_scatter(
        running.reshape(lax.axis_size("dp") * TOK_DEV, RMAX), "dp", scatter_dimension=0, tiled=True
    )
    up_out = jnp.take(adapter_up, expected_output, axis=0)
    up_panels = lax.all_to_all(up_out, "dp", split_axis=1, concat_axis=1, tiled=True)
    up_panels = up_panels.reshape(REQ_DEV, RMAX, -1)
    return finish_rows(base_rows, shrunk, onehot, adapter_ranks, up_panels)


def flip(me, step, n):
    total, weight = 0, 1
    while weight < n:
        total = total + weight * ((me // weight + step // weight) % 2)
        weight *= 2
    return total


AHEAD = 3


def fused(
    n, req,
    adapters_in, lengths_in, ranks_in, tokens, weight, down, up, code,
    out,
    adapters, lengths, ranks, tok, wgt, dwn, upv, codev, base, tok_in, up_out, up_in, part, got,
    load_sem, wgt_sem, tok_send, tok_recv, up_send, up_recv, sum_send, sum_recv,
):
    me = lax.axis_index("dp")
    rows, width = tokens.shape
    chunk = width // n
    far = n // 2
    group, half = up_in.shape[1:]

    loads = [
        pltpu.make_async_copy(source, target, load_sem.at[k])
        for k, (source, target) in enumerate((
            (up, upv), (adapters_in, adapters), (lengths_in, lengths), (ranks_in, ranks),
            (tokens, tok), (down, dwn), (code, codev),
        ))
    ]

    def weight_copy(c):
        piece = pl.ds(pl.multiple_of(c * chunk, chunk), chunk)
        return pltpu.make_async_copy(weight.at[piece], wgt.at[piece], wgt_sem.at[c])

    def token_copy(step):
        peer = flip(me, step, n)
        return pltpu.make_async_remote_copy(
            src_ref=tokens.at[:, pl.ds(pl.multiple_of(peer * chunk, chunk), chunk)],
            dst_ref=tok_in.at[step],
            send_sem=tok_send.at[step], recv_sem=tok_recv.at[step],
            device_id={"dp": peer}, device_id_type=MESH,
        )

    def up_copy(step, arriving=False):
        peer = flip(me, step, n)
        return pltpu.make_async_remote_copy(
            src_ref=up_out.at[peer], dst_ref=up_in.at[peer if arriving else me],
            send_sem=up_send.at[step], recv_sem=up_recv.at[step],
            device_id={"dp": peer}, device_id_type=MESH,
        )

    def sum_copy(level, k):
        slot = n - (n >> level) + k
        return pltpu.make_async_remote_copy(
            src_ref=part.at[(2 * k + 1) << level], dst_ref=got.at[slot],
            send_sem=sum_send.at[slot], recv_sem=sum_recv.at[slot],
            device_id={"dp": flip(me, 1 << level, n)}, device_id_type=MESH,
        )

    barrier = pltpu.get_barrier_semaphore()

    def greet(step, carry):
        pl.semaphore_signal(barrier, inc=1, device_id={"dp": flip(me, step, n)}, device_id_type=MESH)
        return carry

    lax.fori_loop(1, n, greet, 0)
    for load in loads:
        load.start()

    def start_weight(c, carry):
        weight_copy(c).start()
        return carry

    lax.fori_loop(0, n, start_weight, 0)
    pl.semaphore_wait(barrier, n - 1)
    for t in range(AHEAD):
        token_copy(far + t).start()
        if t:
            token_copy(t).start()

    for load in loads[:4]:
        load.wait()

    def pick_up(i, carry):
        panels = [upv[adapters[q, i]].astype(jnp.float32) for q in range(req)]
        picked = [p[:, h * half:(h + 1) * half] for h in range(2) for p in panels]
        up_out[i] = jnp.concatenate(picked, axis=0).astype(jnp.bfloat16)
        return carry

    lax.fori_loop(0, n, pick_up, 0)
    up_in[me] = up_out[me]

    row = lax.broadcasted_iota(jnp.int32, (rows, 1), 0)

    def shrink(step):
        i = flip(me, step, n)
        block = tok_in[step]
        total = jnp.dot(block, dwn[adapters[0, i]], preferred_element_type=jnp.float32)
        end = jnp.int32(0)
        for q in range(1, req):
            end = end + lengths[q - 1, i]
            product = jnp.dot(block, dwn[adapters[q, i]], preferred_element_type=jnp.float32)
            total = jnp.where(row >= end, product, total)
        part[step] = total

    def add_base(c, carry):
        weight_copy(c).wait()
        piece = pl.ds(pl.multiple_of(c * chunk, chunk), chunk)
        base[...] += jnp.dot(tok[:, piece], wgt[piece, :], preferred_element_type=jnp.float32)
        return carry

    ready, moving, sent = set(), [], []

    def mark(level, block):
        ready.add((level, block))
        k = block // 2
        if (1 << level) < n and {(level, 2 * k), (level, 2 * k + 1)} <= ready:
            sum_copy(level, k).start()
            moving.append((level, k))
            sent.append((level, k))

    def absorb():
        level, k = moving.pop(0)
        sum_copy(level, k).wait_recv()
        kept = (2 * k) << level
        part[kept] = part[kept] + got[n - (n >> level) + k]
        mark(level + 1, k)

    ups = list(range(far, n))
    for t in range(far):
        for _ in range(len(moving)):
            absorb()
        if t == 0:
            for load in loads[4:]:
                load.wait()
            tok_in[0] = tok[:, pl.ds(pl.multiple_of(me * chunk, chunk), chunk)]
            base[...] = jnp.zeros_like(base)
        else:
            up_copy(t).start()
            token_copy(t).wait_recv()
        if t + AHEAD < far:
            token_copy(t + AHEAD).start()
        lax.fori_loop(2 * t, 2 * t + 2, add_base, 0)
        token_copy(far + t).wait_recv()
        if t + AHEAD < far:
            token_copy(far + t + AHEAD).start()
        else:
            for step in ups if t == far - 1 else ups[:2]:
                up_copy(step).start()
            ups = ups[2:]

        def one(u, carry):
            shrink(t + u * far)
            return carry

        lax.fori_loop(0, 2, one, 0)
        mark(0, t)
        mark(0, far + t)
    while moving:
        absorb()
    shrunk = part[0]

    request = jnp.zeros((rows, 1), jnp.int32)
    rank = jnp.zeros((rows, 1), jnp.int32) + ranks[adapters[0, me]]
    end = jnp.int32(0)
    for q in range(1, req):
        end = end + lengths[q - 1, me]
        later = row >= end
        request = jnp.where(later, q, request)
        rank = jnp.where(later, ranks[adapters[q, me]], rank)
    within = lax.broadcasted_iota(jnp.int32, shrunk.shape, 1) < rank
    factor = 32.0 / rank.astype(jnp.float32)
    scaled = jnp.where(within, shrunk * factor, 0.0).astype(jnp.bfloat16)
    span = far * group
    codes = codev[0:1, 0:span]
    rank_index = lax.broadcasted_iota(jnp.int32, (shrunk.shape[1], span), 0)

    def await_up(step, carry):
        up_copy(step, arriving=True).wait_recv()
        return carry

    near_side = me // far
    for side, steps in ((near_side, (1, far)), (1 - near_side, (far, n))):
        rank_of = codev[1:2, pl.ds(pl.multiple_of(side * span, span), span)]
        picked = jnp.where(rank_index == rank_of, 1.0, 0.0).astype(jnp.bfloat16)
        spread_out = jnp.dot(scaled, picked, preferred_element_type=jnp.float32)
        placed = [
            jnp.where(codes == request + h * req, spread_out, 0.0).astype(jnp.bfloat16) for h in range(2)
        ]
        lax.fori_loop(*steps, await_up, 0)
        panels = up_in[pl.ds(side * far, far)].reshape(span, half)
        for h in range(2):
            piece = slice(h * half, (h + 1) * half)
            total = base[:, piece] + jnp.dot(placed[h], panels, preferred_element_type=jnp.float32)
            if steps[0] == 1:
                base[:, piece] = total
            else:
                out[:, piece] = total.astype(jnp.bfloat16)

    def await_sent(step, carry):
        token_copy(step).wait_send()
        up_copy(step).wait_send()
        return carry

    lax.fori_loop(1, n, await_sent, 0)
    for pair in sent:
        sum_copy(*pair).wait_send()


def fused_local(tokens, weight, down, up, ranks, adapters, lengths):
    n = lax.axis_size("dp")
    rows, width = tokens.shape
    chunk = width // n
    columns = weight.shape[1]
    req = adapters.shape[1]
    rank_rows, rmax = up.shape[1], down.shape[2]
    half = columns // 2
    group = 2 * req * rank_rows
    spread = n * group
    slot = np.arange(spread)
    rank_of = (slot // group) * rank_rows + slot % rank_rows
    code = np.zeros((8, spread), np.int32)
    code[0], code[1] = (slot % group) // rank_rows, rank_of
    code = jnp.asarray(code)
    dma = pltpu.SemaphoreType.DMA
    return pl.pallas_call(
        functools.partial(fused, n, req),
        out_shape=jax.ShapeDtypeStruct((rows, columns), jnp.bfloat16),
        in_specs=[pl.BlockSpec(memory_space=pl.ANY)] * 8,
        out_specs=pl.BlockSpec(memory_space=pltpu.VMEM),
        scratch_shapes=[
            pltpu.SMEM(adapters.shape[::-1], jnp.int32),
            pltpu.SMEM(lengths.shape[::-1], jnp.int32),
            pltpu.SMEM(ranks.shape, jnp.int32),
            pltpu.VMEM((rows, width), jnp.bfloat16),
            pltpu.VMEM(weight.shape, jnp.bfloat16),
            pltpu.VMEM(down.shape, jnp.bfloat16),
            pltpu.VMEM(up.shape, jnp.bfloat16),
            pltpu.VMEM(code.shape, jnp.int32),
            pltpu.VMEM((rows, columns), jnp.float32),
            pltpu.VMEM((n, rows, chunk), jnp.bfloat16),
            pltpu.VMEM((n, group, half), jnp.bfloat16),
            pltpu.VMEM((n, group, half), jnp.bfloat16),
            pltpu.VMEM((n, rows, rmax), jnp.float32),
            pltpu.VMEM((n - 1, rows, rmax), jnp.float32),
            dma((7,)), dma((n,)), dma((n,)), dma((n,)), dma((n,)), dma((n,)), dma((n,)), dma((n,)),
        ],
        compiler_params=pltpu.CompilerParams(
            collective_id=0, has_side_effects=True, vmem_limit_bytes=56 * 1024 * 1024
        ),
        cost_estimate=pl.CostEstimate(flops=3 * 10**9, bytes_accessed=4 * 10**7, transcendentals=0),
    )(adapters.T, lengths.T, ranks, tokens, weight, down, up, code)


def fits(mesh, tokens, up):
    n = mesh.shape["dp"]
    chunk, rank_rows = tokens.shape[1] // n, up.shape[1] // n
    return n >= 8 and n & (n - 1) == 0 and n <= 32 and chunk % 128 == 0 and rank_rows % 8 == 0


def solution(mesh):
    in_specs = (
        P(("group", "dp"), None),
        P(),
        P("group", "dp", None),
        P("group", "dp", None),
        P("group"),
        P("group", None),
        P("group", None),
    )
    out_specs = P(("group", "dp"), None)

    def run(*arrays):
        body = fused_local if fits(mesh, arrays[0], arrays[3]) else local
        return jax.shard_map(body, mesh=mesh, in_specs=in_specs, out_specs=out_specs, check_vma=False)(*arrays)

    return run
```

time: 90.4 us -> 78.3 us (0.87)
  Pallas kernels: 85.8 us -> 76.5 us
  local copies, waits for them, and re-layouts: 4.37 us -> 1.67 us
    pallas_call x1, Pallas kernels: 85.8 us -> 76.5 us  [fused_local(): pl.pallas_call(functools.partial(fused, n, req), out_shape=jax.ShapeDtype...]
    unnamed x3 -> x1, local copies, waits for them, and re-layouts: 4.37 us -> 1.67 us
where the time goes in v2:
time: 78.3 us; the launch traced here: 78.2 us
  Pallas kernels  76.5 us (98%)
  local copies, waits for them, and re-layouts  1.67 us (2%)
    pallas_call x1, Pallas kernels, fused_local(): pl.pallas_call(functools.partial(fused, n, req), out_shape=jax.ShapeDtype...  76.5 us
    unnamed x1, local copies, waits for them, and re-layouts  1.67 us

profile of v2, /device:TPU:0, one launch (start us, length us, event | category | flops | bytes accessed | tf_op | source)
XLA Modules:
  0.0 78.2 jit_solution(5788812787677874797)
XLA Ops:
  0.0 76.5 %shard_map.82 = bf16[128,1024]{1,0:T(8,128)(2,1)} custom-call(s32[3,16]{1,0:T(4,128)} %bitcast.2, s32[3,16]{1,0:T(4,128)} %bitcast.3, s32[128]{0:T(128)} %ranks_in.1, bf16[128,8192]{1,0:T(8,128)(2,1)} %tokens.1, bf16[8192,1024]{1,0:T(8,128)(2,1)} %weight.1, bf16[128,512,128]{2,1,0:T(8,128)(2,1)} %down.1, bf16[128,8,1024]{2,1,0:T(8,128)(2,1)} %up.1, ...), custom_call_target="tpu_custom_call" | custom-call | flops 3000000000 | bytes 40000000 | tf_op jit(solution)/shard_map/pallas_call | solution.py:318
  76.5 1.7 %copy.10 = bf16[128,1024]{1,0:T(8,128)(2,1)} copy(bf16[128,1024]{1,0:T(8,128)(2,1)} %shard_map.82) | data formatting | bytes 524288

commit v3 on v2

--- a/solution.py
+++ b/solution.py
@@ -96,7 +96,7 @@
     return total
 
 
-AHEAD = 3
+AHEAD = 2
 
 
 def fused(
@@ -167,8 +167,9 @@
     pl.semaphore_wait(barrier, n - 1)
     for t in range(AHEAD):
         token_copy(far + t).start()
-        if t:
-            token_copy(t).start()
+        for step in (2 * t, 2 * t + 1):
+            if step:
+                token_copy(step).start()
 
     for load in loads[:4]:
         load.wait()
@@ -219,7 +220,14 @@
         mark(level + 1, k)
 
     ups = list(range(far, n))
+
+    def start_ups(count):
+        for step in ups[:count]:
+            up_copy(step).start()
+        del ups[:count]
+
     for t in range(far):
+        near = [step for step in (2 * t, 2 * t + 1) if step < far]
         for _ in range(len(moving)):
             absorb()
         if t == 0:
@@ -227,29 +235,34 @@
                 load.wait()
             tok_in[0] = tok[:, pl.ds(pl.multiple_of(me * chunk, chunk), chunk)]
             base[...] = jnp.zeros_like(base)
-        else:
+        for step in near:
+            if step:
+                token_copy(step).wait_recv()
+            if step + 2 * AHEAD < far:
+                token_copy(step + 2 * AHEAD).start()
+        if t:
             up_copy(t).start()
-            token_copy(t).wait_recv()
-        if t + AHEAD < far:
-            token_copy(t + AHEAD).start()
         lax.fori_loop(2 * t, 2 * t + 2, add_base, 0)
+        if near:
+            def one(step, carry):
+                shrink(step)
+                return carry
+
+            lax.fori_loop(near[0], near[-1] + 1, one, 0)
+            for step in near:
+                mark(0, step)
         token_copy(far + t).wait_recv()
         if t + AHEAD < far:
             token_copy(far + t + AHEAD).start()
         else:
-            for step in ups if t == far - 1 else ups[:2]:
-                up_copy(step).start()
-            ups = ups[2:]
-
-        def one(u, carry):
-            shrink(t + u * far)
-            return carry
-
-        lax.fori_loop(0, 2, one, 0)
-        mark(0, t)
+            start_ups(t + AHEAD + 1 - far)
+        shrink(far + t)
         mark(0, far + t)
+    start_ups(2)
     while moving:
         absorb()
+        start_ups(2)
+    start_ups(n)
     shrunk = part[0]
 
     request = jnp.zeros((rows, 1), jnp.int32)

time: 78.3 us -> 77.3 us (0.987)
  Pallas kernels: 76.5 us -> 75.4 us
    pallas_call x1, Pallas kernels: 76.5 us -> 75.4 us  [fused_local(): pl.pallas_call(functools.partial(fused, n, req), out_shape=jax.ShapeDtype...]
where the time goes in v3:
time: 77.3 us; the launch traced here: 77.1 us
  Pallas kernels  75.4 us (98%)
  local copies, waits for them, and re-layouts  1.67 us (2%)
    pallas_call x1, Pallas kernels, fused_local(): pl.pallas_call(functools.partial(fused, n, req), out_shape=jax.ShapeDtype...  75.4 us
    unnamed x1, local copies, waits for them, and re-layouts  1.67 us

profile of v3, /device:TPU:0, one launch (start us, length us, event | category | flops | bytes accessed | tf_op | source)
XLA Modules:
  0.0 77.1 jit_solution(12998423394929833254)
XLA Ops:
  0.0 75.4 %shard_map.82 = bf16[128,1024]{1,0:T(8,128)(2,1)} custom-call(s32[3,16]{1,0:T(4,128)} %bitcast.2, s32[3,16]{1,0:T(4,128)} %bitcast.3, s32[128]{0:T(128)} %ranks_in.1, bf16[128,8192]{1,0:T(8,128)(2,1)} %tokens.1, bf16[8192,1024]{1,0:T(8,128)(2,1)} %weight.1, bf16[128,512,128]{2,1,0:T(8,128)(2,1)} %down.1, bf16[128,8,1024]{2,1,0:T(8,128)(2,1)} %up.1, ...), custom_call_target="tpu_custom_call" | custom-call | flops 3000000000 | bytes 40000000 | tf_op jit(solution)/shard_map/pallas_call | solution.py:331
  75.5 1.7 %copy.10 = bf16[128,1024]{1,0:T(8,128)(2,1)} copy(bf16[128,1024]{1,0:T(8,128)(2,1)} %shard_map.82) | data formatting | bytes 524288

commit v4 on v3

--- a/solution.py
+++ b/solution.py
@@ -166,7 +166,7 @@
     lax.fori_loop(0, n, start_weight, 0)
     pl.semaphore_wait(barrier, n - 1)
     for t in range(AHEAD):
-        token_copy(far + t).start()
+        token_copy(n - 1 - t).start()
         for step in (2 * t, 2 * t + 1):
             if step:
                 token_copy(step).start()
@@ -207,10 +207,11 @@
     def mark(level, block):
         ready.add((level, block))
         k = block // 2
-        if (1 << level) < n and {(level, 2 * k), (level, 2 * k + 1)} <= ready:
+        if block % 2:
             sum_copy(level, k).start()
+            sent.append((level, k))
+        if {(level, 2 * k), (level, 2 * k + 1)} <= ready:
             moving.append((level, k))
-            sent.append((level, k))
 
     def absorb():
         level, k = moving.pop(0)
@@ -251,18 +252,18 @@
             lax.fori_loop(near[0], near[-1] + 1, one, 0)
             for step in near:
                 mark(0, step)
-        token_copy(far + t).wait_recv()
+        last = n - 1 - t
+        token_copy(last).wait_recv()
         if t + AHEAD < far:
-            token_copy(far + t + AHEAD).start()
+            token_copy(last - AHEAD).start()
         else:
-            start_ups(t + AHEAD + 1 - far)
-        shrink(far + t)
-        mark(0, far + t)
-    start_ups(2)
+            start_ups(2)
+        shrink(last)
+        mark(0, last)
     while moving:
+        if moving[0][0] == n.bit_length() - 2:
+            start_ups(n)
         absorb()
-        start_ups(2)
-    start_ups(n)
     shrunk = part[0]
 
     request = jnp.zeros((rows, 1), jnp.int32)

time: 77.3 us -> 74.9 us (0.969)
  the two profiles are of different devices: /device:TPU:0 before, /device:TPU:9 now
where the time goes in v4:
time: 74.9 us; the launch traced here: 74.8 us
  Pallas kernels  73.1 us (98%)
  local copies, waits for them, and re-layouts  1.67 us (2%)
    pallas_call x1, Pallas kernels, fused_local(): pl.pallas_call(functools.partial(fused, n, req), out_shape=jax.ShapeDtype...  73.1 us
    unnamed x1, local copies, waits for them, and re-layouts  1.67 us

profile of v4, /device:TPU:9, one launch (start us, length us, event | category | flops | bytes accessed | tf_op | source)
XLA Modules:
  0.0 74.8 jit_solution(14645950342964619232)
XLA Ops:
  0.0 73.1 %shard_map.82 = bf16[128,1024]{1,0:T(8,128)(2,1)} custom-call(s32[3,16]{1,0:T(4,128)} %bitcast.2, s32[3,16]{1,0:T(4,128)} %bitcast.3, s32[128]{0:T(128)} %ranks_in.1, bf16[128,8192]{1,0:T(8,128)(2,1)} %tokens.1, bf16[8192,1024]{1,0:T(8,128)(2,1)} %weight.1, bf16[128,512,128]{2,1,0:T(8,128)(2,1)} %down.1, bf16[128,8,1024]{2,1,0:T(8,128)(2,1)} %up.1, ...), custom_call_target="tpu_custom_call" | custom-call | flops 3000000000 | bytes 40000000 | tf_op jit(solution)/shard_map/pallas_call | solution.py:332
  73.1 1.7 %copy.10 = bf16[128,1024]{1,0:T(8,128)(2,1)} copy(bf16[128,1024]{1,0:T(8,128)(2,1)} %shard_map.82) | data formatting | bytes 524288

commit v5 on v4

--- a/solution.py
+++ b/solution.py
@@ -96,7 +96,7 @@
     return total
 
 
-AHEAD = 2
+AHEAD = 3
 
 
 def fused(
@@ -257,7 +257,7 @@
         if t + AHEAD < far:
             token_copy(last - AHEAD).start()
         else:
-            start_ups(2)
+            start_ups(1 if t + AHEAD == far else 2)
         shrink(last)
         mark(0, last)
     while moving:

time: 74.9 us -> 74.2 us (level)
  the two profiles are of different devices: /device:TPU:9 before, /device:TPU:11 now
where the time goes in v5:
time: 74.2 us; the launch traced here: 74.1 us
  Pallas kernels  72.4 us (98%)
  local copies, waits for them, and re-layouts  1.67 us (2%)
    pallas_call x1, Pallas kernels, fused_local(): pl.pallas_call(functools.partial(fused, n, req), out_shape=jax.ShapeDtype...  72.4 us
    unnamed x1, local copies, waits for them, and re-layouts  1.67 us

profile of v5, /device:TPU:11, one launch (start us, length us, event | category | flops | bytes accessed | tf_op | source)
XLA Modules:
  0.0 74.1 jit_solution(8138730983830653786)
XLA Ops:
  0.0 72.4 %shard_map.82 = bf16[128,1024]{1,0:T(8,128)(2,1)} custom-call(s32[3,16]{1,0:T(4,128)} %bitcast.2, s32[3,16]{1,0:T(4,128)} %bitcast.3, s32[128]{0:T(128)} %ranks_in.1, bf16[128,8192]{1,0:T(8,128)(2,1)} %tokens.1, bf16[8192,1024]{1,0:T(8,128)(2,1)} %weight.1, bf16[128,512,128]{2,1,0:T(8,128)(2,1)} %down.1, bf16[128,8,1024]{2,1,0:T(8,128)(2,1)} %up.1, ...), custom_call_target="tpu_custom_call" | custom-call | flops 3000000000 | bytes 40000000 | tf_op jit(solution)/shard_map/pallas_call | solution.py:332
  72.4 1.7 %copy.10 = bf16[128,1024]{1,0:T(8,128)(2,1)} copy(bf16[128,1024]{1,0:T(8,128)(2,1)} %shard_map.82) | data formatting | bytes 524288
